TPU v7x, 768 devices: a whole 4x8x12 slice. The times are simulated.
768 devices in a mesh: space: 64 (over z_hi, y, core), ens: 12 (over z_lo, x).
Axes of the slice: x: 4, y: 8, z: 12 (z_hi: 4, z_lo: 3; z = z_hi * 3 + z_lo), core: 2. Of those that a mesh axis runs over, the one named last changes fastest.
Arguments:
- members: bfloat16 [96, 8, 196608], P('ens', None, 'space'), may hold values from -6 to 6
- field: bfloat16 [8, 196608], P(None, 'space'), may hold values from -6 to 6
- weight: bfloat16 [1536, 4, 128, 128], P('space'), may hold values from -0.25 to 0.25
- offsets: int32 [1536, 4], P('space'), may hold values from -2 to 2
Outputs:
- increment: float32 [8, 196608], P(None, 'space')
All inputs are finite; a program needn't handle non-finite values.
Results may differ from a plain program's by a relative error of at most 0.00077.
Values may be sent and summed in bfloat16 or wider, within the bound.
A program may use at most 32 MiB of HBM per device.

v0:
```python
import jax
import jax.numpy as jnp
from jax import lax
from jax.sharding import PartitionSpec as P

BS = 128
HALO = 2


def padded(cells, sides, width):
    for axis, dim in sides:
        count = lax.axis_size(axis)
        head = lax.slice_in_dim(cells, 0, width, axis=dim)
        tail = lax.slice_in_dim(cells, cells.shape[dim] - width, cells.shape[dim], axis=dim)
        cells = jnp.concatenate(
            [
                lax.ppermute(tail, axis, [(i, (i + 1) % count) for i in range(count)]),
                cells,
                lax.ppermute(head, axis, [((i + 1) % count, i) for i in range(count)]),
            ],
            axis=dim,
        )
    return cells


def spread_back(scaled, weight, offsets):
    product = jnp.einsum("rbd,btcd->rbtc", scaled, weight, preferred_element_type=jnp.float32)
    total = None
    for reach in range(-HALO, HALO + 1):
        select = (offsets == reach).astype(jnp.float32)[None, :, :, None]
        slab = jnp.sum(product * select, axis=2)
        placed = jnp.pad(slab, ((0, 0), (HALO + reach, HALO - reach), (0, 0)))
        total = placed if total is None else total + placed
    return total


def spread_out(extended, weight, offsets):
    block_count = weight.shape[0]
    positions = jnp.arange(block_count, dtype=jnp.int32)[:, None] + HALO + offsets
    chosen = jnp.take(extended, positions, axis=1)
    return jnp.einsum("rbtc,btcd->rbd", chosen, weight, preferred_element_type=jnp.float32)


def settle(core, arrived):
    block_count = core.shape[1]
    from_left = arrived[:, :HALO]
    from_right = arrived[:, 3 * HALO :]
    core = core.at[:, :HALO].add(from_left)
    core = core.at[:, block_count - HALO :].add(from_right)
    return core.astype(jnp.bfloat16)


def tile_rims_back(lower, upper):
    joined = jnp.concatenate([lower, upper], axis=1)
    return padded(joined.astype(jnp.bfloat16), (("space", 1),), HALO).astype(joined.dtype)


def tile_rims(spread):
    return padded(spread, (("space", 1),), HALO)


def local(members, field, weight, offsets):
    member_count, channel_count, cell_total = members.shape
    block_count = weight.shape[0]
    scaled = (members.astype(jnp.float32) * field.astype(jnp.float32)[None]).astype(jnp.bfloat16)
    scaled = scaled.reshape(member_count * channel_count, block_count, BS)
    total = spread_back(scaled, weight, offsets)
    arrived = tile_rims_back(total[:, :HALO], total[:, block_count + HALO :])
    spread = settle(total[:, HALO : HALO + block_count], arrived)
    extended = tile_rims(spread)
    ahead = spread_out(extended, weight, offsets)
    ahead = ahead.reshape(member_count, channel_count, cell_total)
    partial_sum = jnp.sum(members.astype(jnp.float32) * ahead, axis=0)
    return lax.psum(partial_sum, "ens")


def solution(mesh):
    in_specs = (
        P("ens", None, "space"),
        P(None, "space"),
        P("space", None, None, None),
        P("space", None),
    )
    out_specs = P(None, "space")
    return jax.shard_map(local, mesh=mesh, in_specs=in_specs, out_specs=out_specs, check_vma=False)
```

profile of v0, /device:TPU:192, one launch (start us, length us, event | category | flops | bytes accessed | tf_op | source)
XLA Modules:
  0.0 205.4 jit_solution(17633820231169043382)
XLA Ops:
  6.5 0.8 compare_and_fusion
  7.4 0.1 copy.15
  7.5 0.1 copy.16
  7.6 0.1 copy.17
  7.6 0.1 copy.18
  7.7 0.1 copy.19
  7.8 0.8 convert_element_type.43
  8.6 1.1 fusion.10
  9.8 2.3 %multiply_reduce_fusion.4 = (f32[24,64,128]{2,1,0:T(8,128)S(1)}, f32[24,64,128]{2,1,0:T(8,128)S(1)}, f32[24,64,128]{2,1,0:T(8,128)S(1)}, f32[24,64,128]{2,1,0:T(8,128)S(1)}, f32[24,64,128]{2,1,0:T(8,128)S(1)}) fusion(f32[24,4]{1,0:T(8,128)S(1)} %copy.15, f32[24,4]{1,0:T(8,128)S(1)} %copy.19, f32[24,4]{1,0:T(8,128)S(1)} %copy.18, f32[24,4]{1,0:T(8,128)S(1)} %copy.17, ...), kind=kOutput, calls=%fused_computation.5 | convolution fusion | flops 208207872 | bytes 7473024 | tf_op jit(solution)/shard_map/rbd,btcd->rbtc/dot_general | solution.py:27
  12.1 0.5 fusion.16
  12.6 1.9 collective-permute-start
  14.5 7.5 %collective-permute-start.1 = (bf16[64,2,128]{2,0,1:T(8,128)(2,1)S(1)}, bf16[64,2,128]{2,0,1:T(8,128)(2,1)S(1)}, u32[]{:S(2)}, u32[]{:S(2)}) collective-permute-start(bf16[64,2,128]{2,0,1:T(8,128)(2,1)S(1)} %get-tuple-element.39), channel_id=1, source_target_pairs={{12,0},{24,12},{36,24},{48,36},{60,48},{72,60},{84,72},{96,84},{10... | collective-permute-start | bytes 98312 | tf_op jit(solution)/shard_map/ppermute | solution.py:19
  22.1 1.0 slice.85
  23.1 0.1 copy.20
  23.1 0.1 reshape.86
  23.2 0.4 collective-permute-done.1
  23.7 1.5 fusion.14
  25.1 1.5 fusion.13
  26.6 1.2 convert_element_type.51
  27.8 0.6 fusion.18
  28.4 1.9 collective-permute-start.2
  30.3 7.6 %collective-permute-start.3 = (bf16[64,2,128]{2,0,1:T(8,128)(2,1)}, bf16[64,2,128]{2,0,1:T(8,128)(2,1)}, u32[]{:S(2)}, u32[]{:S(2)}) collective-permute-start(bf16[64,2,128]{2,0,1:T(8,128)(2,1)} %get-tuple-element.41), channel_id=1, source_target_pairs={{12,0},{24,12},{36,24},{48,36},{60,48},{72,60},{84,72},{96,84},{10... | collective-permute-start | bytes 98312 | tf_op jit(solution)/shard_map/ppermute | solution.py:19
  37.9 0.1 copy.13
  38.0 1.8 collective-permute-done.3
  39.8 1.6 pad_maximum_fusion
  41.4 3.0 %gather_fusion = bf16[96,64,128]{2,1,0:T(8,128)(2,1)} fusion(bf16[64,28,128]{2,0,1:T(8,128)(2,1)} %pad_maximum_fusion, s32[1024]{0:T(1024)S(1)} %pad_clamp_fusion), kind=kCustom, calls=%fused_computation | custom fusion | bytes 3146112 | tf_op jit(solution)/shard_map/jit(_take)/gather | solution.py:40
  44.4 2.2 %fusion.4 = f32[64,24,128]{2,0,1:T(8,128)S(1)} fusion(bf16[24,4,128,128]{3,2,1,0:T(8,128)(2,1)S(1)} %copy-done, bf16[24,4,64,128]{3,2,1,0:T(8,128)(2,1)} %bitcast.24, pred[24,4]{1,0:T(8,128)(4,1)S(1)} %copy.13), kind=kOutput, calls=%fused_computation.10 | convolution fusion | flops 202113024 | bytes 5505120 | tf_op jit(solution)/shard_map/rbtc,btcd->rbd/dot_general | solution.py:41
  46.6 1.3 copy.21
  47.9 2.2 %reshape.83 = f32[8,8,3072]{2,1,0:T(8,128)} reshape(f32[64,24,128]{2,1,0:T(8,128)} %copy.21) | data formatting | bytes 1572864 | tf_op jit(solution)/shard_map/reshape | solution.py:72
  50.1 1.9 fusion.8
  52.0 145.0 %all-reduce.7.cloned.1.call-done = f32[8,3072]{1,0:T(8,128)} async-done(((f32[8,3072]{1,0:T(8,128)}), f32[8,3072]{1,0:T(8,128)}) %all-reduce.7.cloned.1.call-update) | async-done | bytes 98320 | tf_op jit(solution)/shard_map/psum | solution.py:74
  197.0 1.5 copy.34
  (14 shorter events, 0.1 us)
Async XLA Ops:
  6.5 3.2 %copy-start = (bf16[24,4,128,128]{3,2,1,0:T(8,128)(2,1)S(1)}, bf16[24,4,128,128]{3,2,1,0:T(8,128)(2,1)}, u32[]{:S(2)}) copy-start(bf16[24,4,128,128]{3,2,1,0:T(8,128)(2,1)} %param.10) | copy-start | bytes 9437188
  6.5 190.4 %all-reduce.7.cloned.1.call-start = ((), (), s32[]{:S(2)}) async-start(), calls=%async_computation | async-start | bytes 196608 | tf_op jit(solution)/shard_map/psum | solution.py:74
  12.6 9.5 %copy-start.1 = (f32[64,28,128]{2,0,1:T(8,128)}, f32[64,28,128]{2,0,1:T(8,128)S(1)}, u32[]{:S(2)}) copy-start(f32[64,28,128]{2,0,1:T(8,128)S(1)} %get-tuple-element.37) | copy-start | bytes 2752516
  12.6 10.6 %collective-permute-start = (bf16[64,2,128]{2,0,1:T(8,128)(2,1)S(1)}, bf16[64,2,128]{2,0,1:T(8,128)(2,1)S(1)}, u32[]{:S(2)}, u32[]{:S(2)}) collective-permute-start(bf16[64,2,128]{2,0,1:T(8,128)(2,1)S(1)} %get-tuple-element.38), channel_id=1, source_target_pairs={{0,12},{12,24},{24,36},{36,48},{48,60},{60,72},{72,84},{84,96},{96... | collective-permute-start | bytes 98312 | tf_op jit(solution)/shard_map/ppermute | solution.py:17
  14.5 9.1 %collective-permute-start.1 = (bf16[64,2,128]{2,0,1:T(8,128)(2,1)S(1)}, bf16[64,2,128]{2,0,1:T(8,128)(2,1)S(1)}, u32[]{:S(2)}, u32[]{:S(2)}) collective-permute-start(bf16[64,2,128]{2,0,1:T(8,128)(2,1)S(1)} %get-tuple-element.39), channel_id=1, source_target_pairs={{12,0},{24,12},{36,24},{48,36},{60,48},{72,60},{84,72},{96,84},{10... | collective-permute-start | bytes 98312 | tf_op jit(solution)/shard_map/ppermute | solution.py:19
  28.4 9.6 %collective-permute-start.2 = (bf16[64,2,128]{2,0,1:T(8,128)(2,1)}, bf16[64,2,128]{2,0,1:T(8,128)(2,1)}, u32[]{:S(2)}, u32[]{:S(2)}) collective-permute-start(bf16[64,2,128]{2,0,1:T(8,128)(2,1)} %get-tuple-element.40), channel_id=1, source_target_pairs={{0,12},{12,24},{24,36},{36,48},{48,60},{60,72},{72,84},{84,96},{96... | collective-permute-start | bytes 98312 | tf_op jit(solution)/shard_map/ppermute | solution.py:17
  30.3 9.5 %collective-permute-start.3 = (bf16[64,2,128]{2,0,1:T(8,128)(2,1)}, bf16[64,2,128]{2,0,1:T(8,128)(2,1)}, u32[]{:S(2)}, u32[]{:S(2)}) collective-permute-start(bf16[64,2,128]{2,0,1:T(8,128)(2,1)} %get-tuple-element.41), channel_id=1, source_target_pairs={{12,0},{24,12},{36,24},{48,36},{60,48},{72,60},{84,72},{96,84},{10... | collective-permute-start | bytes 98312 | tf_op jit(solution)/shard_map/ppermute | solution.py:19
  44.4 5.7 %copy-start.2 = (bf16[8,8,3072]{2,1,0:T(8,128)(2,1)S(1)}, bf16[8,8,3072]{2,1,0:T(8,128)(2,1)}, u32[]{:S(2)}) copy-start(bf16[8,8,3072]{2,1,0:T(8,128)(2,1)} %param.8) | copy-start | bytes 1179652
Sparse Core Ops, SparseCore 0:
  52.1 144.8 all-reduce.6
where the time goes:
time: 206 us; the launch traced here: 205 us
  waiting for transfers between devices  147 us (71%)
  starting transfers between devices  18.9 us (9%)
  between operations  13.5 us (7%)
  other arithmetic  10.8 us (5%)
  local copies, waits for them, and re-layouts  10.4 us (5%)
  matrix products  4.55 us (2%)
    psum x1, waiting for transfers between devices, local(): return lax.psum(partial_sum, 'ens')  145 us
    ppermute x2, starting transfers between devices, padded(): lax.ppermute(head, axis, [((i + 1) % count, i) for i in range(count)])  15.1 us
  transfers between devices with their start and end apart: 5, of which 3 were waited for; matrix products, arithmetic and copies ran while one was open for 1% of the time, Pallas kernels for 0%

commit v1 on v0

v1 whole, which is shorter than its diff:
```python
import functools

import jax
import jax.numpy as jnp
from jax import lax
from jax.experimental import pallas as pl
from jax.experimental.pallas import tpu as pltpu
from jax.sharding import PartitionSpec as P

BS = 128
HALO = 2
TAPS = 4
RIM = 2 * HALO
MESH = pl.DeviceIdType.MESH


def kernel(
    n_space, n_ens, nb, rows, ch,
    offsets_ref, members_hbm, field_hbm, weight_hbm, out_ref,
    members, field, weight, back, spread, rim_out, rim_in, part, parts_in,
    in_sems, weight_sems, rim_send, rim_recv, rs_send, rs_recv, ag_send, ag_recv,
):
    me_s = lax.axis_index("space")
    me_e = lax.axis_index("ens")
    right = lax.rem(me_s + 1, n_space)
    left = lax.rem(me_s + n_space - 1, n_space)
    chunks = nb // RIM
    order = [0, chunks - 1] + list(range(1, chunks - 1))

    members_copy = pltpu.make_async_copy(members_hbm, members, in_sems.at[0])
    field_copy = pltpu.make_async_copy(field_hbm, field, in_sems.at[1])
    members_copy.start()
    field_copy.start()
    weight_copies = {}
    for c in order:
        piece = pl.ds(c * RIM, RIM)
        weight_copies[c] = pltpu.make_async_copy(weight_hbm.at[piece], weight.at[piece], weight_sems.at[c])
        weight_copies[c].start()

    barrier = pltpu.get_barrier_semaphore()
    for neighbour in (left, right):
        pl.semaphore_signal(barrier, inc=1, device_id=(neighbour, me_e), device_id_type=MESH)

    def greet(k, _):
        pl.semaphore_signal(barrier, inc=1, device_id=(me_s, lax.rem(me_e + k, n_ens)), device_id_type=MESH)
        return 0

    lax.fori_loop(1, n_ens, greet, 0)

    back[...] = jnp.zeros_like(back)

    def cells(b):
        return pl.ds(pl.multiple_of(b * BS, BS), BS)

    def adjoint(b, _):
        m = members[:, cells(b)].astype(jnp.float32).reshape(rows // ch, ch, BS)
        f = field[:, cells(b)].astype(jnp.float32)
        scaled = (m * f[None]).astype(jnp.bfloat16).reshape(rows, BS)
        product = lax.dot_general(
            scaled, weight[b], (((1,), (1,)), ((), ())), preferred_element_type=jnp.float32
        )
        taps = [offsets_ref[t, b] for t in range(TAPS)]
        for reach in range(-HALO, HALO + 1):
            slab = None
            for t in range(TAPS):
                term = jnp.where(taps[t] == reach, product[:, t * BS : (t + 1) * BS], 0.0)
                slab = term if slab is None else slab + term
            back[b + HALO + reach] += slab
        return 0

    def forward(b, _):
        total = None
        for t in range(TAPS):
            source = spread[b + HALO + offsets_ref[t, b]]
            term = jnp.dot(source, weight[b, t * BS : (t + 1) * BS, :], preferred_element_type=jnp.float32)
            total = term if total is None else total + term
        m = members[:, cells(b)].astype(jnp.float32).reshape(rows // ch, ch, BS)
        return jnp.sum(m * total.reshape(rows // ch, ch, BS), axis=0)

    def forward_pair(p):
        part[p, 0] = forward(2 * p, 0)
        part[p, 1] = forward(2 * p + 1, 0)

        @pl.when(p != me_e)
        def _():
            slot = lax.rem(p - me_e + n_ens, n_ens) - 1
            pltpu.make_async_remote_copy(
                src_ref=part.at[p], dst_ref=parts_in.at[slot],
                send_sem=rs_send, recv_sem=rs_recv,
                device_id=(me_s, p), device_id_type=MESH,
            ).start()

    members_copy.wait()
    field_copy.wait()
    weight_copies[0].wait()
    lax.fori_loop(0, RIM, adjoint, 0)
    rim_out[0] = back[0:RIM].astype(jnp.bfloat16)
    weight_copies[chunks - 1].wait()
    lax.fori_loop(nb - RIM, nb, adjoint, 0)
    rim_out[1] = back[nb : nb + RIM].astype(jnp.bfloat16)

    pl.semaphore_wait(barrier, n_ens + 1)
    rims = []
    for side, target in ((0, left), (1, right)):
        copy = pltpu.make_async_remote_copy(
            src_ref=rim_out.at[side], dst_ref=rim_in.at[side],
            send_sem=rim_send.at[side], recv_sem=rim_recv.at[side],
            device_id=(target, me_e), device_id_type=MESH,
        )
        copy.start()
        rims.append(copy)

    for c in range(1, chunks - 1):
        weight_copies[c].wait()
        lax.fori_loop(c * RIM, (c + 1) * RIM, adjoint, 0)

    spread[RIM:nb] = back[RIM:nb].astype(jnp.bfloat16)

    def inner(p, _):
        forward_pair(p)
        return 0

    lax.fori_loop(RIM // 2, (nb - RIM) // 2, inner, 0)

    rims[0].wait()
    rims[1].wait()
    spread[0:RIM] = (back[0:RIM] + rim_in[1].astype(jnp.float32)).astype(jnp.bfloat16)
    spread[nb : nb + RIM] = (back[nb : nb + RIM] + rim_in[0].astype(jnp.float32)).astype(jnp.bfloat16)
    lax.fori_loop(0, RIM // 2, inner, 0)
    lax.fori_loop((nb - RIM) // 2, nb // 2, inner, 0)

    all_in = pltpu.make_async_copy(parts_in, parts_in, rs_recv)
    all_in.wait()
    total = part[me_e]
    for k in range(n_ens - 1):
        total = total + parts_in[k]
    width = 2 * BS
    mine = pl.ds(pl.multiple_of(me_e * width, width), width)
    out_ref[:, mine] = jnp.concatenate([total[0], total[1]], axis=1)

    def give(k, _):
        pltpu.make_async_remote_copy(
            src_ref=out_ref.at[:, mine], dst_ref=out_ref.at[:, mine],
            send_sem=ag_send, recv_sem=ag_recv,
            device_id=(me_s, lax.rem(me_e + k, n_ens)), device_id_type=MESH,
        ).start()
        return 0

    lax.fori_loop(1, n_ens, give, 0)
    pltpu.make_async_copy(parts_in, parts_in, ag_recv).wait()
    pltpu.make_async_copy(parts_in, parts_in, rs_send).wait()
    pltpu.make_async_copy(parts_in, parts_in, ag_send).wait()


def local(n_space, n_ens, members, field, weight, offsets):
    member_count, ch, cell_total = members.shape
    nb = weight.shape[0]
    rows = member_count * ch
    dma = pltpu.SemaphoreType.DMA
    call = pl.pallas_call(
        functools.partial(kernel, n_space, n_ens, nb, rows, ch),
        out_shape=jax.ShapeDtypeStruct((ch, cell_total), jnp.float32),
        in_specs=[
            pl.BlockSpec(memory_space=pltpu.SMEM),
            pl.BlockSpec(memory_space=pl.ANY),
            pl.BlockSpec(memory_space=pl.ANY),
            pl.BlockSpec(memory_space=pl.ANY),
        ],
        out_specs=pl.BlockSpec(memory_space=pltpu.VMEM),
        scratch_shapes=[
            pltpu.VMEM((rows, cell_total), jnp.bfloat16),
            pltpu.VMEM((ch, cell_total), jnp.bfloat16),
            pltpu.VMEM((nb, TAPS * BS, BS), jnp.bfloat16),
            pltpu.VMEM((nb + RIM, rows, BS), jnp.float32),
            pltpu.VMEM((nb + RIM, rows, BS), jnp.bfloat16),
            pltpu.VMEM((2, RIM, rows, BS), jnp.bfloat16),
            pltpu.VMEM((2, RIM, rows, BS), jnp.bfloat16),
            pltpu.VMEM((n_ens, 2, ch, BS), jnp.float32),
            pltpu.VMEM((n_ens - 1, 2, ch, BS), jnp.float32),
            dma((2,)),
            dma((nb // RIM,)),
            dma((2,)),
            dma((2,)),
            dma,
            dma,
            dma,
            dma,
        ],
        compiler_params=pltpu.CompilerParams(
            collective_id=0, has_side_effects=True, vmem_limit_bytes=63 * 1024 * 1024
        ),
        cost_estimate=pl.CostEstimate(flops=403_000_000, bytes_accessed=3_800_000, transcendentals=0),
    )
    return call(
        offsets.T,
        members.reshape(rows, cell_total),
        field,
        weight.reshape(nb, TAPS * BS, BS),
    )


def solution(mesh):
    in_specs = (
        P("ens", None, "space"),
        P(None, "space"),
        P("space", None, None, None),
        P("space", None),
    )
    out_specs = P(None, "space")
    body = functools.partial(local, mesh.shape["space"], mesh.shape["ens"])
    return jax.shard_map(body, mesh=mesh, in_specs=in_specs, out_specs=out_specs, check_vma=False)
```

time: 206 us -> 35.3 us (0.17)
  the two profiles are of different devices: /device:TPU:192 before, /device:TPU:2 now
where the time goes in v1:
time: 35.3 us; the launch traced here: 35.1 us
  Pallas kernels  33.6 us (95%)
  local copies, waits for them, and re-layouts  1.54 us (4%)
    pallas_call x1, Pallas kernels, local(): call(offsets.T, members.reshape(rows, cell_total), field, weight.reshape(...  33.6 us
    unnamed x1, local copies, waits for them, and re-layouts  1.54 us

profile of v1, /device:TPU:2, one launch (start us, length us, event | category | flops | bytes accessed | tf_op | source)
XLA Modules:
  0.0 35.1 jit_solution(15164238635630096974)
XLA Ops:
  0.0 33.6 %shard_map.46 = f32[8,3072]{1,0:T(8,128)} custom-call(s32[4,24]{1,0:T(4,128)} %bitcast.5, bf16[64,3072]{1,0:T(8,128)(2,1)} %bitcast.4, bf16[8,3072]{1,0:T(8,128)(2,1)} %field_hbm.1, bf16[24,512,128]{2,1,0:T(8,128)(2,1)} %bitcast.3), custom_call_target="tpu_custom_call" | custom-call | flops 403000000 | bytes 3800000 | tf_op jit(solution)/shard_map/pallas_call | solution.py:194
  33.6 1.5 %copy.6 = f32[8,3072]{1,0:T(8,128)} copy(f32[8,3072]{1,0:T(8,128)} %shard_map.46) | data formatting | bytes 196608

commit v2 on v1

--- a/solution.py
+++ b/solution.py
@@ -11,6 +11,7 @@
 HALO = 2
 TAPS = 4
 RIM = 2 * HALO
+VMEM_LIMIT = 32 * 1024 * 1024
 MESH = pl.DeviceIdType.MESH
 
 
@@ -50,9 +51,9 @@
     back[...] = jnp.zeros_like(back)
 
     def cells(b):
-        return pl.ds(pl.multiple_of(b * BS, BS), BS)
-
-    def adjoint(b, _):
+        return pl.ds(b * BS, BS)
+
+    def adjoint(b):
         m = members[:, cells(b)].astype(jnp.float32).reshape(rows // ch, ch, BS)
         f = field[:, cells(b)].astype(jnp.float32)
         scaled = (m * f[None]).astype(jnp.bfloat16).reshape(rows, BS)
@@ -66,9 +67,8 @@
                 term = jnp.where(taps[t] == reach, product[:, t * BS : (t + 1) * BS], 0.0)
                 slab = term if slab is None else slab + term
             back[b + HALO + reach] += slab
-        return 0
-
-    def forward(b, _):
+
+    def forward(b):
         total = None
         for t in range(TAPS):
             source = spread[b + HALO + offsets_ref[t, b]]
@@ -78,8 +78,8 @@
         return jnp.sum(m * total.reshape(rows // ch, ch, BS), axis=0)
 
     def forward_pair(p):
-        part[p, 0] = forward(2 * p, 0)
-        part[p, 1] = forward(2 * p + 1, 0)
+        part[p, 0] = forward(2 * p)
+        part[p, 1] = forward(2 * p + 1)
 
         @pl.when(p != me_e)
         def _():
@@ -93,10 +93,12 @@
     members_copy.wait()
     field_copy.wait()
     weight_copies[0].wait()
-    lax.fori_loop(0, RIM, adjoint, 0)
+    for b in range(RIM):
+        adjoint(b)
     rim_out[0] = back[0:RIM].astype(jnp.bfloat16)
     weight_copies[chunks - 1].wait()
-    lax.fori_loop(nb - RIM, nb, adjoint, 0)
+    for b in range(nb - RIM, nb):
+        adjoint(b)
     rim_out[1] = back[nb : nb + RIM].astype(jnp.bfloat16)
 
     pl.semaphore_wait(barrier, n_ens + 1)
@@ -112,22 +114,20 @@
 
     for c in range(1, chunks - 1):
         weight_copies[c].wait()
-        lax.fori_loop(c * RIM, (c + 1) * RIM, adjoint, 0)
+        for b in range(c * RIM, (c + 1) * RIM):
+            adjoint(b)
 
     spread[RIM:nb] = back[RIM:nb].astype(jnp.bfloat16)
 
-    def inner(p, _):
+    for p in range(RIM // 2, (nb - RIM) // 2):
         forward_pair(p)
-        return 0
-
-    lax.fori_loop(RIM // 2, (nb - RIM) // 2, inner, 0)
 
     rims[0].wait()
     rims[1].wait()
     spread[0:RIM] = (back[0:RIM] + rim_in[1].astype(jnp.float32)).astype(jnp.bfloat16)
     spread[nb : nb + RIM] = (back[nb : nb + RIM] + rim_in[0].astype(jnp.float32)).astype(jnp.bfloat16)
-    lax.fori_loop(0, RIM // 2, inner, 0)
-    lax.fori_loop((nb - RIM) // 2, nb // 2, inner, 0)
+    for p in (*range(RIM // 2), *range((nb - RIM) // 2, nb // 2)):
+        forward_pair(p)
 
     all_in = pltpu.make_async_copy(parts_in, parts_in, rs_recv)
     all_in.wait()
@@ -159,12 +159,12 @@
     dma = pltpu.SemaphoreType.DMA
     call = pl.pallas_call(
         functools.partial(kernel, n_space, n_ens, nb, rows, ch),
-        out_shape=jax.ShapeDtypeStruct((ch, cell_total), jnp.float32),
+        out_shape=pltpu.VMEM((ch, cell_total), jnp.float32),
         in_specs=[
             pl.BlockSpec(memory_space=pltpu.SMEM),
-            pl.BlockSpec(memory_space=pl.ANY),
-            pl.BlockSpec(memory_space=pl.ANY),
-            pl.BlockSpec(memory_space=pl.ANY),
+            pl.BlockSpec(memory_space=pltpu.HBM),
+            pl.BlockSpec(memory_space=pltpu.HBM),
+            pl.BlockSpec(memory_space=pltpu.HBM),
         ],
         out_specs=pl.BlockSpec(memory_space=pltpu.VMEM),
         scratch_shapes=[
@@ -187,15 +187,15 @@
             dma,
         ],
         compiler_params=pltpu.CompilerParams(
-            collective_id=0, has_side_effects=True, vmem_limit_bytes=63 * 1024 * 1024
+            collective_id=0, has_side_effects=True, vmem_limit_bytes=VMEM_LIMIT
         ),
         cost_estimate=pl.CostEstimate(flops=403_000_000, bytes_accessed=3_800_000, transcendentals=0),
     )
     return call(
-        offsets.T,
-        members.reshape(rows, cell_total),
-        field,
-        weight.reshape(nb, TAPS * BS, BS),
+        pltpu.with_memory_space_constraint(offsets.T, pltpu.HBM),
+        pltpu.with_memory_space_constraint(members.reshape(rows, cell_total), pltpu.HBM),
+        pltpu.with_memory_space_constraint(field, pltpu.HBM),
+        pltpu.with_memory_space_constraint(weight.reshape(nb, TAPS * BS, BS), pltpu.HBM),
     )
 
 

time: 35.3 us -> 33.4 us (0.946)
  Pallas kernels: 33.6 us -> 32.6 us
  local copies, waits for them, and re-layouts: 1.54 us -> 0.64 us
    pallas_call x1, Pallas kernels: 33.6 us -> 32.6 us  [local(): call(pltpu.with_memory_space_constraint(offsets.T, pltpu.HBM), pltpu.with...]
    unnamed x1, local copies, waits for them, and re-layouts: 1.54 us -> 0.64 us
where the time goes in v2:
time: 33.4 us; the launch traced here: 33.2 us
  Pallas kernels  32.6 us (98%)
  local copies, waits for them, and re-layouts  0.64 us (2%)
    pallas_call x1, Pallas kernels, local(): call(pltpu.with_memory_space_constraint(offsets.T, pltpu.HBM), pltpu.with...  32.6 us

profile of v2, /device:TPU:2, one launch (start us, length us, event | category | flops | bytes accessed | tf_op | source)
XLA Modules:
  0.0 33.2 jit_solution(9972329717535248087)
XLA Ops:
  0.0 32.6 %shard_map.46 = f32[8,3072]{1,0:T(8,128)S(1)} custom-call(s32[4,24]{1,0:T(4,128)} %bitcast.5, bf16[64,3072]{1,0:T(8,128)(2,1)} %bitcast.4, bf16[8,3072]{1,0:T(8,128)(2,1)} %field_hbm.1, bf16[24,512,128]{2,1,0:T(8,128)(2,1)} %bitcast.3), custom_call_target="tpu_custom_call" | custom-call | flops 403000000 | bytes 3800000 | tf_op jit(solution)/shard_map/pallas_call | solution.py:194
  32.6 0.6 %copy.6 = f32[8,3072]{1,0:T(8,128)} copy(f32[8,3072]{1,0:T(8,128)S(1)} %shard_map.46) | data formatting | bytes 196608

commit v3 on v2

v3 whole, which is shorter than its diff:
```python
import functools

import jax
import jax.numpy as jnp
from jax import lax
from jax.experimental import pallas as pl
from jax.experimental.pallas import tpu as pltpu
from jax.sharding import PartitionSpec as P

BS = 128
HALO = 2
TAPS = 4
RIM = 2 * HALO
ROW = 4
MESH = pl.DeviceIdType.MESH
VMEM_LIMIT = 32 * 1024 * 1024


def kernel(
    n_space, n_ens, nb, rows, ch,
    offsets_hbm, members_hbm, field_hbm, weight_hbm, out_ref,
    offsets, members, field, weight, back, spread, rim_out, rim_in, part, parts_in, border,
    in_sems, weight_sems, ready, rim_send, rim_recv, rs_send, rs_recv, ag_send, ag_recv, border_send, border_recv,
):
    me_s = lax.axis_index("space")
    me_e = lax.axis_index("ens")
    right = lax.rem(me_s + 1, n_space)
    left = lax.rem(me_s + n_space - 1, n_space)
    first = me_s == 0
    last = me_s == n_space - 1
    chunks = nb // RIM
    inner = chunks - 2
    order = [0, chunks - 1] + list(range(1, chunks - 1))

    partners = []
    for dx in (2, 1, 3, 0):
        for dz in (1, 2, 0):
            if dx or dz:
                z = lax.rem(me_e // ROW + dz, n_ens // ROW)
                partners.append(z * ROW + lax.rem(lax.rem(me_e, ROW) + dx, ROW))

    def owner(g):
        return ROW + g

    loads = [
        pltpu.make_async_copy(members_hbm, members, in_sems.at[0]),
        pltpu.make_async_copy(field_hbm, field, in_sems.at[1]),
        pltpu.make_async_copy(offsets_hbm, offsets, in_sems.at[2]),
    ]
    for copy in loads:
        copy.start()
    weight_copies = {}
    for c in order:
        piece = pl.ds(c * RIM, RIM)
        weight_copies[c] = pltpu.make_async_copy(weight_hbm.at[piece], weight.at[piece], weight_sems.at[c])
        weight_copies[c].start()

    barrier = pltpu.get_barrier_semaphore()

    @pl.when(jnp.logical_not(last))
    def _():
        pl.semaphore_signal(barrier, inc=1, device_id=(right, me_e), device_id_type=MESH)

    @pl.when(first)
    def _():
        pl.semaphore_signal(barrier, inc=1, device_id=(left, me_e), device_id_type=MESH)

    for p in partners:
        pl.semaphore_signal(barrier, inc=1, device_id=(me_s, p), device_id_type=MESH)

    back[...] = jnp.zeros_like(back)

    def cells(b):
        return pl.ds(b * BS if isinstance(b, int) else pl.multiple_of(b * BS, BS), BS)

    def adjoint(b):
        m = members[:, cells(b)].astype(jnp.float32).reshape(rows // ch, ch, BS)
        f = field[:, cells(b)].astype(jnp.float32)
        scaled = (m * f[None]).astype(jnp.bfloat16).reshape(rows, BS)
        product = lax.dot_general(
            scaled, weight[b], (((1,), (1,)), ((), ())), preferred_element_type=jnp.float32
        )
        taps = [offsets[t, b] for t in range(TAPS)]
        for reach in range(-HALO, HALO + 1):
            slab = None
            for t in range(TAPS):
                term = jnp.where(taps[t] == reach, product[:, t * BS : (t + 1) * BS], 0.0)
                slab = term if slab is None else slab + term
            back[b + HALO + reach] += slab

    def forward(b):
        total = None
        for t in range(TAPS):
            source = spread[b + HALO + offsets[t, b]]
            term = jnp.dot(source, weight[b, t * BS : (t + 1) * BS, :], preferred_element_type=jnp.float32)
            total = term if total is None else total + term
        m = members[:, cells(b)].astype(jnp.float32).reshape(rows // ch, ch, BS)
        return jnp.sum(m * total.reshape(rows // ch, ch, BS), axis=0)

    def send_rim(side):
        pltpu.make_async_remote_copy(
            src_ref=rim_out.at[side], dst_ref=rim_in.at[1 - side],
            send_sem=rim_send.at[side], recv_sem=rim_recv.at[1 - side],
            device_id=(right if side else left, me_e), device_id_type=MESH,
        ).start()

    def wait_for(ref, sem):
        pltpu.make_async_copy(ref, ref, sem).wait()

    for copy in loads:
        copy.wait()
    weight_copies[0].wait()
    for b in range(RIM):
        adjoint(b)
    rim_out[0] = back[0:RIM].astype(jnp.bfloat16)
    weight_copies[chunks - 1].wait()
    for b in range(nb - RIM, nb):
        adjoint(b)
    rim_out[1] = back[nb : nb + RIM].astype(jnp.bfloat16)

    pl.semaphore_wait(barrier, n_ens - 1 + jnp.where(first, 0, 1) + jnp.where(last, 1, 0))

    @pl.when(jnp.logical_not(first))
    def _():
        send_rim(0)
        pl.semaphore_signal(ready.at[1], inc=1, device_id=(left, me_e), device_id_type=MESH)

    @pl.when(last)
    def _():
        send_rim(1)
        pl.semaphore_signal(ready.at[0], inc=1, device_id=(right, me_e), device_id_type=MESH)

    for c in range(1, chunks - 1):
        weight_copies[c].wait()
        for b in range(c * RIM, (c + 1) * RIM):
            adjoint(b)

    spread[RIM:nb] = back[RIM:nb].astype(jnp.bfloat16)

    for g in range(inner):
        for i in range(RIM):
            part[g, i] = forward(RIM * (g + 1) + i)

        @pl.when(me_e != owner(g))
        def _():
            slot = lax.rem(owner(g) - me_e + n_ens, n_ens) - 1
            pltpu.make_async_remote_copy(
                src_ref=part.at[g], dst_ref=parts_in.at[slot],
                send_sem=rs_send.at[g], recv_sem=rs_recv,
                device_id=(me_s, owner(g)), device_id_type=MESH,
            ).start()

    @pl.when(jnp.logical_not(last))
    def _():
        pl.semaphore_wait(ready.at[1], 1)
        send_rim(1)

    def finish_border(side):
        base = side * (nb - RIM)
        rim = pl.ds(side * nb, RIM)
        wait_for(rim_in.at[side], rim_recv.at[side])
        spread[rim] = (back[rim] + rim_in[side].astype(jnp.float32)).astype(jnp.bfloat16)
        for i in range(RIM):
            border[side, me_e, i] = forward(base + i)
        for p in partners:
            pltpu.make_async_remote_copy(
                src_ref=border.at[side, me_e], dst_ref=border.at[side, me_e],
                send_sem=border_send.at[side], recv_sem=border_recv.at[side],
                device_id=(me_s, p), device_id_type=MESH,
            ).start()

    near = 1 - lax.rem(me_s, 2)
    far = 1 - near
    finish_border(near)

    @pl.when(first)
    def _():
        pl.semaphore_wait(ready.at[0], 1)
        send_rim(0)

    width = RIM * BS
    owns = jnp.logical_and(me_e >= owner(0), me_e < owner(inner))

    @pl.when(owns)
    def _():
        wait_for(parts_in, rs_recv)
        g = me_e - owner(0)
        total = part[g]
        for k in range(n_ens - 1):
            total = total + parts_in[k]
        mine = pl.ds(pl.multiple_of((g + 1) * width, width), width)
        out_ref[:, mine] = jnp.concatenate([total[i] for i in range(RIM)], axis=1)
        for p in partners:
            pltpu.make_async_remote_copy(
                src_ref=out_ref.at[:, mine], dst_ref=out_ref.at[:, mine],
                send_sem=ag_send, recv_sem=ag_recv.at[g],
                device_id=(me_s, p), device_id_type=MESH,
            ).start()

    finish_border(far)

    for side in (0, 1):
        wait_for(border.at[side, 0 : n_ens - 1], border_recv.at[side])
        total = border[side, 0]
        for k in range(1, n_ens):
            total = total + border[side, k]
        start = side * (nb - RIM) * BS
        out_ref[:, start : start + width] = jnp.concatenate([total[i] for i in range(RIM)], axis=1)

    for g in range(inner):

        @pl.when(me_e != owner(g))
        def _():
            wait_for(out_ref.at[:, pl.ds((g + 1) * width, width)], ag_recv.at[g])
            wait_for(part.at[g], rs_send.at[g])

    @pl.when(owns)
    def _():
        wait_for(parts_in, ag_send)

    for side in (0, 1):
        wait_for(rim_out.at[side], rim_send.at[side])
        wait_for(border.at[side, 0 : n_ens - 1], border_send.at[side])


def local(n_space, n_ens, members, field, weight, offsets):
    member_count, ch, cell_total = members.shape
    nb = weight.shape[0]
    rows = member_count * ch
    inner = nb // RIM - 2
    dma = pltpu.SemaphoreType.DMA
    call = pl.pallas_call(
        functools.partial(kernel, n_space, n_ens, nb, rows, ch),
        out_shape=pltpu.VMEM((ch, cell_total), jnp.float32),
        in_specs=[pl.BlockSpec(memory_space=pltpu.HBM)] * 4,
        out_specs=pl.BlockSpec(memory_space=pltpu.VMEM),
        scratch_shapes=[
            pltpu.SMEM((TAPS, nb), jnp.int32),
            pltpu.VMEM((rows, cell_total), jnp.bfloat16),
            pltpu.VMEM((ch, cell_total), jnp.bfloat16),
            pltpu.VMEM((nb, TAPS * BS, BS), jnp.bfloat16),
            pltpu.VMEM((nb + RIM, rows, BS), jnp.float32),
            pltpu.VMEM((nb + RIM, rows, BS), jnp.bfloat16),
            pltpu.VMEM((2, RIM, rows, BS), jnp.bfloat16),
            pltpu.VMEM((2, RIM, rows, BS), jnp.bfloat16),
            pltpu.VMEM((inner, RIM, ch, BS), jnp.float32),
            pltpu.VMEM((n_ens - 1, RIM, ch, BS), jnp.float32),
            pltpu.VMEM((2, n_ens, RIM, ch, BS), jnp.float32),
            dma((3,)),
            dma((nb // RIM,)),
            pltpu.SemaphoreType.REGULAR((2,)),
            dma((2,)),
            dma((2,)),
            dma((inner,)),
            dma,
            dma,
            dma((inner,)),
            dma((2,)),
            dma((2,)),
        ],
        compiler_params=pltpu.CompilerParams(
            collective_id=0, has_side_effects=True, vmem_limit_bytes=VMEM_LIMIT
        ),
        cost_estimate=pl.CostEstimate(flops=403_000_000, bytes_accessed=3_800_000, transcendentals=0),
    )
    operands = (
        offsets.T,
        members.reshape(rows, cell_total),
        field,
        weight.reshape(nb, TAPS * BS, BS),
    )
    return call(*(pltpu.with_memory_space_constraint(x, pltpu.HBM) for x in operands))


def solution(mesh):
    in_specs = (
        P("ens", None, "space"),
        P(None, "space"),
        P("space", None, None, None),
        P("space", None),
    )
    out_specs = P(None, "space")
    body = functools.partial(local, mesh.shape["space"], mesh.shape["ens"])
    return jax.shard_map(body, mesh=mesh, in_specs=in_specs, out_specs=out_specs, check_vma=False)
```

time: 33.4 us -> 28.7 us (0.86)
  Pallas kernels: 32.6 us -> 27.9 us
    pallas_call x1, Pallas kernels: 32.6 us -> 27.9 us  [local(): call(*(pltpu.with_memory_space_constraint(x, pltpu.HBM) for x in operands))]
where the time goes in v3:
time: 28.7 us; the launch traced here: 28.6 us
  Pallas kernels  27.9 us (97%)
  local copies, waits for them, and re-layouts  0.64 us (2%)
    pallas_call x1, Pallas kernels, local(): call(*(pltpu.with_memory_space_constraint(x, pltpu.HBM) for x in operands))  27.9 us
    unnamed x1, local copies, waits for them, and re-layouts  0.64 us

profile of v3, /device:TPU:2, one launch (start us, length us, event | category | flops | bytes accessed | tf_op | source)
XLA Modules:
  0.0 28.6 jit_solution(5176586654351686522)
XLA Ops:
  0.0 27.9 %shard_map.46 = f32[8,3072]{1,0:T(8,128)S(1)} custom-call(s32[4,24]{1,0:T(4,128)} %bitcast.5, bf16[64,3072]{1,0:T(8,128)(2,1)} %bitcast.4, bf16[8,3072]{1,0:T(8,128)(2,1)} %field_hbm.1, bf16[24,512,128]{2,1,0:T(8,128)(2,1)} %bitcast.3), custom_call_target="tpu_custom_call" | custom-call | flops 403000000 | bytes 3800000 | tf_op jit(solution)/shard_map/pallas_call | solution.py:272
  27.9 0.6 %copy.6 = f32[8,3072]{1,0:T(8,128)} copy(f32[8,3072]{1,0:T(8,128)S(1)} %shard_map.46) | data formatting | bytes 196608

commit v4 on v3

--- a/solution.py
+++ b/solution.py
@@ -20,7 +20,7 @@
     n_space, n_ens, nb, rows, ch,
     offsets_hbm, members_hbm, field_hbm, weight_hbm, out_ref,
     offsets, members, field, weight, back, spread, rim_out, rim_in, part, parts_in, border,
-    in_sems, weight_sems, ready, rim_send, rim_recv, rs_send, rs_recv, ag_send, ag_recv, border_send, border_recv,
+    in_sems, weight_sems, ready, met, rim_send, rim_recv, rs_send, rs_recv, ag_send, ag_recv, border_send, border_recv,
 ):
     me_s = lax.axis_index("space")
     me_e = lax.axis_index("ens")
@@ -30,14 +30,17 @@
     last = me_s == n_space - 1
     chunks = nb // RIM
     inner = chunks - 2
-    order = [0, chunks - 1] + list(range(1, chunks - 1))
-
+    order = [chunks - 1, 0] + list(range(1, chunks - 1))
+
+    row, x = me_e // ROW, lax.rem(me_e, ROW)
+    away = jnp.where(row == 0, 2, 1)
     partners = []
-    for dx in (2, 1, 3, 0):
-        for dz in (1, 2, 0):
-            if dx or dz:
-                z = lax.rem(me_e // ROW + dz, n_ens // ROW)
-                partners.append(z * ROW + lax.rem(lax.rem(me_e, ROW) + dx, ROW))
+    for dz in (away, n_ens // ROW - away, 0):
+        for dx in (2, 1, 3, 0):
+            if dx or not isinstance(dz, int):
+                partners.append(lax.rem(row + dz, n_ens // ROW) * ROW + lax.rem(x + dx, ROW))
+    cross = [row * ROW + lax.rem(x + dx, ROW) for dx in range(1, ROW)]
+    cross += [lax.rem(row + dz, n_ens // ROW) * ROW + x for dz in range(1, n_ens // ROW)]
 
     def owner(g):
         return ROW + g
@@ -65,7 +68,7 @@
     def _():
         pl.semaphore_signal(barrier, inc=1, device_id=(left, me_e), device_id_type=MESH)
 
-    for p in partners:
+    for p in cross:
         pl.semaphore_signal(barrier, inc=1, device_id=(me_s, p), device_id_type=MESH)
 
     back[...] = jnp.zeros_like(back)
@@ -109,16 +112,16 @@
 
     for copy in loads:
         copy.wait()
+    weight_copies[chunks - 1].wait()
+    for b in range(nb - RIM, nb):
+        adjoint(b)
+    rim_out[1] = back[nb : nb + RIM].astype(jnp.bfloat16)
     weight_copies[0].wait()
     for b in range(RIM):
         adjoint(b)
     rim_out[0] = back[0:RIM].astype(jnp.bfloat16)
-    weight_copies[chunks - 1].wait()
-    for b in range(nb - RIM, nb):
-        adjoint(b)
-    rim_out[1] = back[nb : nb + RIM].astype(jnp.bfloat16)
-
-    pl.semaphore_wait(barrier, n_ens - 1 + jnp.where(first, 0, 1) + jnp.where(last, 1, 0))
+
+    pl.semaphore_wait(barrier, len(cross) + jnp.where(first, 0, 1) + jnp.where(last, 1, 0))
 
     @pl.when(jnp.logical_not(first))
     def _():
@@ -129,6 +132,9 @@
     def _():
         send_rim(1)
         pl.semaphore_signal(ready.at[0], inc=1, device_id=(right, me_e), device_id_type=MESH)
+
+    for p in cross:
+        pl.semaphore_signal(met, inc=1, device_id=(me_s, p), device_id_type=MESH)
 
     for c in range(1, chunks - 1):
         weight_copies[c].wait()
@@ -137,6 +143,7 @@
 
     spread[RIM:nb] = back[RIM:nb].astype(jnp.bfloat16)
 
+    pl.semaphore_wait(met, len(cross))
     for g in range(inner):
         for i in range(RIM):
             part[g, i] = forward(RIM * (g + 1) + i)
@@ -173,11 +180,6 @@
     far = 1 - near
     finish_border(near)
 
-    @pl.when(first)
-    def _():
-        pl.semaphore_wait(ready.at[0], 1)
-        send_rim(0)
-
     width = RIM * BS
     owns = jnp.logical_and(me_e >= owner(0), me_e < owner(inner))
 
@@ -197,16 +199,23 @@
                 device_id=(me_s, p), device_id_type=MESH,
             ).start()
 
+    @pl.when(first)
+    def _():
+        pl.semaphore_wait(ready.at[0], 1)
+        send_rim(0)
+
     finish_border(far)
 
-    for side in (0, 1):
+    def sum_border(side):
         wait_for(border.at[side, 0 : n_ens - 1], border_recv.at[side])
         total = border[side, 0]
         for k in range(1, n_ens):
             total = total + border[side, k]
-        start = side * (nb - RIM) * BS
-        out_ref[:, start : start + width] = jnp.concatenate([total[i] for i in range(RIM)], axis=1)
-
+        columns = pl.ds(pl.multiple_of(side * (nb - RIM) * BS, width), width)
+        out_ref[:, columns] = jnp.concatenate([total[i] for i in range(RIM)], axis=1)
+        wait_for(border.at[side, 0 : n_ens - 1], border_send.at[side])
+
+    sum_border(near)
     for g in range(inner):
 
         @pl.when(me_e != owner(g))
@@ -220,7 +229,7 @@
 
     for side in (0, 1):
         wait_for(rim_out.at[side], rim_send.at[side])
-        wait_for(border.at[side, 0 : n_ens - 1], border_send.at[side])
+    sum_border(far)
 
 
 def local(n_space, n_ens, members, field, weight, offsets):
@@ -249,6 +258,7 @@
             dma((3,)),
             dma((nb // RIM,)),
             pltpu.SemaphoreType.REGULAR((2,)),
+            pltpu.SemaphoreType.REGULAR,
             dma((2,)),
             dma((2,)),
             dma((inner,)),

time: 28.7 us -> 28.5 us (level)
  no operation moved by 1% of the time
where the time goes in v4:
time: 28.5 us; the launch traced here: 28.4 us
  Pallas kernels  27.7 us (97%)
  local copies, waits for them, and re-layouts  0.64 us (2%)
    pallas_call x1, Pallas kernels, local(): call(*(pltpu.with_memory_space_constraint(x, pltpu.HBM) for x in operands))  27.7 us
    unnamed x1, local copies, waits for them, and re-layouts  0.64 us

profile of v4, /device:TPU:2, one launch (start us, length us, event | category | flops | bytes accessed | tf_op | source)
XLA Modules:
  0.0 28.4 jit_solution(15196733876404985427)
XLA Ops:
  0.0 27.7 %shard_map.46 = f32[8,3072]{1,0:T(8,128)S(1)} custom-call(s32[4,24]{1,0:T(4,128)} %bitcast.5, bf16[64,3072]{1,0:T(8,128)(2,1)} %bitcast.4, bf16[8,3072]{1,0:T(8,128)(2,1)} %field_hbm.1, bf16[24,512,128]{2,1,0:T(8,128)(2,1)} %bitcast.3), custom_call_target="tpu_custom_call" | custom-call | flops 403000000 | bytes 3800000 | tf_op jit(solution)/shard_map/pallas_call | solution.py:282
  27.8 0.6 %copy.6 = f32[8,3072]{1,0:T(8,128)} copy(f32[8,3072]{1,0:T(8,128)S(1)} %shard_map.46) | data formatting | bytes 196608

commit v5 on v4

--- a/solution.py
+++ b/solution.py
@@ -20,7 +20,7 @@
     n_space, n_ens, nb, rows, ch,
     offsets_hbm, members_hbm, field_hbm, weight_hbm, out_ref,
     offsets, members, field, weight, back, spread, rim_out, rim_in, part, parts_in, border,
-    in_sems, weight_sems, ready, met, rim_send, rim_recv, rs_send, rs_recv, ag_send, ag_recv, border_send, border_recv,
+    in_sems, member_sems, weight_sems, ready, met, rim_send, rim_recv, rs_send, rs_recv, ag_send, ag_recv, border_send, border_recv,
 ):
     me_s = lax.axis_index("space")
     me_e = lax.axis_index("ens")
@@ -28,6 +28,8 @@
     left = lax.rem(me_s + n_space - 1, n_space)
     first = me_s == 0
     last = me_s == n_space - 1
+    ends = jnp.logical_or(first, last)
+    tail = me_s >= n_space - 2
     chunks = nb // RIM
     inner = chunks - 2
     order = [chunks - 1, 0] + list(range(1, chunks - 1))
@@ -46,25 +48,36 @@
         return ROW + g
 
     loads = [
-        pltpu.make_async_copy(members_hbm, members, in_sems.at[0]),
+        pltpu.make_async_copy(offsets_hbm, offsets, in_sems.at[2]),
         pltpu.make_async_copy(field_hbm, field, in_sems.at[1]),
-        pltpu.make_async_copy(offsets_hbm, offsets, in_sems.at[2]),
     ]
     for copy in loads:
         copy.start()
-    weight_copies = {}
+    member_copies, weight_copies = {}, {}
+    pieces = {chunks - 1: (chunks - 1, chunks), 0: (0, 1), 1: (1, chunks - 1)}
     for c in order:
+        if c in pieces:
+            low, high = pieces[c]
+            columns = pl.ds(low * RIM * BS, (high - low) * RIM * BS)
+            member_copies[c] = pltpu.make_async_copy(members_hbm.at[:, columns], members.at[:, columns], member_sems.at[len(member_copies)])
         piece = pl.ds(c * RIM, RIM)
         weight_copies[c] = pltpu.make_async_copy(weight_hbm.at[piece], weight.at[piece], weight_sems.at[c])
+
+    def load(c):
+        if c in member_copies:
+            member_copies[c].start()
         weight_copies[c].start()
 
+    load(chunks - 1)
+    load(0)
+
     barrier = pltpu.get_barrier_semaphore()
 
-    @pl.when(jnp.logical_not(last))
+    @pl.when(jnp.logical_not(tail))
     def _():
         pl.semaphore_signal(barrier, inc=1, device_id=(right, me_e), device_id_type=MESH)
 
-    @pl.when(first)
+    @pl.when(ends)
     def _():
         pl.semaphore_signal(barrier, inc=1, device_id=(left, me_e), device_id_type=MESH)
 
@@ -112,31 +125,37 @@
 
     for copy in loads:
         copy.wait()
+    member_copies[chunks - 1].wait()
     weight_copies[chunks - 1].wait()
+    for c in order[2:]:
+        load(c)
     for b in range(nb - RIM, nb):
         adjoint(b)
     rim_out[1] = back[nb : nb + RIM].astype(jnp.bfloat16)
+    pl.semaphore_wait(barrier, len(cross) + jnp.where(ends, 0, 1) + jnp.where(tail, 1, 0))
+
+    @pl.when(tail)
+    def _():
+        send_rim(1)
+        pl.semaphore_signal(ready.at[0], inc=1, device_id=(right, me_e), device_id_type=MESH)
+
+    member_copies[0].wait()
     weight_copies[0].wait()
     for b in range(RIM):
         adjoint(b)
     rim_out[0] = back[0:RIM].astype(jnp.bfloat16)
 
-    pl.semaphore_wait(barrier, len(cross) + jnp.where(first, 0, 1) + jnp.where(last, 1, 0))
-
-    @pl.when(jnp.logical_not(first))
+    @pl.when(jnp.logical_not(ends))
     def _():
         send_rim(0)
         pl.semaphore_signal(ready.at[1], inc=1, device_id=(left, me_e), device_id_type=MESH)
 
-    @pl.when(last)
-    def _():
-        send_rim(1)
-        pl.semaphore_signal(ready.at[0], inc=1, device_id=(right, me_e), device_id_type=MESH)
-
     for p in cross:
         pl.semaphore_signal(met, inc=1, device_id=(me_s, p), device_id_type=MESH)
 
     for c in range(1, chunks - 1):
+        if c in member_copies:
+            member_copies[c].wait()
         weight_copies[c].wait()
         for b in range(c * RIM, (c + 1) * RIM):
             adjoint(b)
@@ -157,7 +176,7 @@
                 device_id=(me_s, owner(g)), device_id_type=MESH,
             ).start()
 
-    @pl.when(jnp.logical_not(last))
+    @pl.when(jnp.logical_not(tail))
     def _():
         pl.semaphore_wait(ready.at[1], 1)
         send_rim(1)
@@ -175,6 +194,11 @@
                 send_sem=border_send.at[side], recv_sem=border_recv.at[side],
                 device_id=(me_s, p), device_id_type=MESH,
             ).start()
+
+    @pl.when(last)
+    def _():
+        pl.semaphore_wait(ready.at[0], 1)
+        send_rim(0)
 
     near = 1 - lax.rem(me_s, 2)
     far = 1 - near
@@ -255,6 +279,7 @@
             pltpu.VMEM((inner, RIM, ch, BS), jnp.float32),
             pltpu.VMEM((n_ens - 1, RIM, ch, BS), jnp.float32),
             pltpu.VMEM((2, n_ens, RIM, ch, BS), jnp.float32),
+            dma((3,)),
             dma((3,)),
             dma((nb // RIM,)),
             pltpu.SemaphoreType.REGULAR((2,)),

time: 28.5 us -> 27.7 us (0.972)
  the two profiles are of different devices: /device:TPU:2 before, /device:TPU:6 now
where the time goes in v5:
time: 27.7 us; the launch traced here: 27.6 us
  Pallas kernels  26.9 us (97%)
  local copies, waits for them, and re-layouts  0.64 us (2%)
    pallas_call x1, Pallas kernels, local(): call(*(pltpu.with_memory_space_constraint(x, pltpu.HBM) for x in operands))  26.9 us
    unnamed x1, local copies, waits for them, and re-layouts  0.64 us

profile of v5, /device:TPU:6, one launch (start us, length us, event | category | flops | bytes accessed | tf_op | source)
XLA Modules:
  0.0 27.6 jit_solution(8516691187983233645)
XLA Ops:
  0.0 26.9 %shard_map.46 = f32[8,3072]{1,0:T(8,128)S(1)} custom-call(s32[4,24]{1,0:T(4,128)} %bitcast.5, bf16[64,3072]{1,0:T(8,128)(2,1)} %bitcast.4, bf16[8,3072]{1,0:T(8,128)(2,1)} %field_hbm.1, bf16[24,512,128]{2,1,0:T(8,128)(2,1)} %bitcast.3), custom_call_target="tpu_custom_call" | custom-call | flops 403000000 | bytes 3800000 | tf_op jit(solution)/shard_map/pallas_call | solution.py:307
  26.9 0.6 %copy.6 = f32[8,3072]{1,0:T(8,128)} copy(f32[8,3072]{1,0:T(8,128)S(1)} %shard_map.46) | data formatting | bytes 196608

commit v6 on v5

--- a/solution.py
+++ b/solution.py
@@ -20,7 +20,9 @@
     n_space, n_ens, nb, rows, ch,
     offsets_hbm, members_hbm, field_hbm, weight_hbm, out_ref,
     offsets, members, field, weight, back, spread, rim_out, rim_in, part, parts_in, border,
+    rims, pack, gift_members, gift_spread, gift_back,
     in_sems, member_sems, weight_sems, ready, met, rim_send, rim_recv, rs_send, rs_recv, ag_send, ag_recv, border_send, border_recv,
+    rims_recv, gift_send, gift_recv,
 ):
     me_s = lax.axis_index("space")
     me_e = lax.axis_index("ens")
@@ -43,6 +45,10 @@
                 partners.append(lax.rem(row + dz, n_ens // ROW) * ROW + lax.rem(x + dx, ROW))
     cross = [row * ROW + lax.rem(x + dx, ROW) for dx in range(1, ROW)]
     cross += [lax.rem(row + dz, n_ens // ROW) * ROW + x for dz in range(1, n_ens // ROW)]
+
+    n_rows = n_ens // ROW
+    giver = jnp.logical_and(first, row > 0)
+    taker = jnp.logical_and(first, row == 0)
 
     def owner(g):
         return ROW + g
@@ -81,6 +87,11 @@
     def _():
         pl.semaphore_signal(barrier, inc=1, device_id=(left, me_e), device_id_type=MESH)
 
+    @pl.when(taker)
+    def _():
+        for r in range(1, n_rows):
+            pl.semaphore_signal(barrier, inc=1, device_id=(left, r * ROW + x), device_id_type=MESH)
+
     for p in cross:
         pl.semaphore_signal(barrier, inc=1, device_id=(me_s, p), device_id_type=MESH)
 
@@ -132,11 +143,23 @@
     for b in range(nb - RIM, nb):
         adjoint(b)
     rim_out[1] = back[nb : nb + RIM].astype(jnp.bfloat16)
-    pl.semaphore_wait(barrier, len(cross) + jnp.where(ends, 0, 1) + jnp.where(tail, 1, 0))
+    pl.semaphore_wait(barrier, len(cross) + jnp.where(ends, 0, 1) + jnp.where(tail, 1, 0)
+        + jnp.where(jnp.logical_and(last, row > 0), 1, 0))
 
     @pl.when(tail)
     def _():
-        send_rim(1)
+        @pl.when(last)
+        def _():
+            pltpu.make_async_remote_copy(
+                src_ref=rim_out.at[1], dst_ref=rims.at[row],
+                send_sem=rim_send.at[1], recv_sem=rims_recv.at[row],
+                device_id=(right, x), device_id_type=MESH,
+            ).start()
+
+        @pl.when(jnp.logical_not(last))
+        def _():
+            send_rim(1)
+
         pl.semaphore_signal(ready.at[0], inc=1, device_id=(right, me_e), device_id_type=MESH)
 
     member_copies[0].wait()
@@ -152,6 +175,28 @@
 
     for p in cross:
         pl.semaphore_signal(met, inc=1, device_id=(me_s, p), device_id_type=MESH)
+
+    @pl.when(first)
+    def _():
+        pl.semaphore_wait(ready.at[1], 1)
+        send_rim(1)
+
+    gifts = (
+        (pack, gift_members),
+        (spread.at[RIM : 2 * RIM], gift_spread),
+        (rim_out.at[0], gift_back),
+    )
+
+    @pl.when(giver)
+    def _():
+        for b in range(RIM):
+            pack[b] = members[:, cells(b)]
+        for i, (mine, gift) in ((0, gifts[0]), (2, gifts[2])):
+            pltpu.make_async_remote_copy(
+                src_ref=mine, dst_ref=gift.at[row - 1],
+                send_sem=gift_send.at[i], recv_sem=gift_recv.at[i, row - 1],
+                device_id=(me_s, x), device_id_type=MESH,
+            ).start()
 
     for c in range(1, chunks - 1):
         if c in member_copies:
@@ -161,6 +206,14 @@
             adjoint(b)
 
     spread[RIM:nb] = back[RIM:nb].astype(jnp.bfloat16)
+
+    @pl.when(giver)
+    def _():
+        pltpu.make_async_remote_copy(
+            src_ref=gifts[1][0], dst_ref=gift_spread.at[row - 1],
+            send_sem=gift_send.at[1], recv_sem=gift_recv.at[1, row - 1],
+            device_id=(me_s, x), device_id_type=MESH,
+        ).start()
 
     pl.semaphore_wait(met, len(cross))
     for g in range(inner):
@@ -176,7 +229,7 @@
                 device_id=(me_s, owner(g)), device_id_type=MESH,
             ).start()
 
-    @pl.when(jnp.logical_not(tail))
+    @pl.when(jnp.logical_not(jnp.logical_or(first, tail)))
     def _():
         pl.semaphore_wait(ready.at[1], 1)
         send_rim(1)
@@ -188,6 +241,9 @@
         spread[rim] = (back[rim] + rim_in[side].astype(jnp.float32)).astype(jnp.bfloat16)
         for i in range(RIM):
             border[side, me_e, i] = forward(base + i)
+        give_border(side)
+
+    def give_border(side):
         for p in partners:
             pltpu.make_async_remote_copy(
                 src_ref=border.at[side, me_e], dst_ref=border.at[side, me_e],
@@ -228,18 +284,44 @@
         pl.semaphore_wait(ready.at[0], 1)
         send_rim(0)
 
-    finish_border(far)
-
-    def sum_border(side):
-        wait_for(border.at[side, 0 : n_ens - 1], border_recv.at[side])
+    @pl.when(jnp.logical_not(first))
+    def _():
+        finish_border(far)
+
+    @pl.when(taker)
+    def _():
+        def finish_row(r, _):
+            wait_for(rims.at[r], rims_recv.at[r])
+
+            @pl.when(r > 0)
+            def _():
+                for i, (mine, gift) in enumerate(gifts):
+                    wait_for(gift.at[r - 1], gift_recv.at[i, r - 1])
+                for b in range(RIM):
+                    members[:, cells(b)] = gift_members[r - 1, b]
+                spread[RIM : 2 * RIM] = gift_spread[r - 1]
+                back[0:RIM] = gift_back[r - 1].astype(jnp.float32)
+
+            spread[0:RIM] = (back[0:RIM] + rims[r].astype(jnp.float32)).astype(jnp.bfloat16)
+            for i in range(RIM):
+                border[0, me_e, i] += forward(i)
+            return 0
+
+        border[0, me_e] = jnp.zeros_like(border[0, me_e])
+        lax.fori_loop(0, n_rows, finish_row, 0)
+        give_border(0)
+
+    def sum_border(side, count=n_ens):
         total = border[side, 0]
-        for k in range(1, n_ens):
+        for k in range(1, count):
             total = total + border[side, k]
         columns = pl.ds(pl.multiple_of(side * (nb - RIM) * BS, width), width)
         out_ref[:, columns] = jnp.concatenate([total[i] for i in range(RIM)], axis=1)
-        wait_for(border.at[side, 0 : n_ens - 1], border_send.at[side])
-
+
+    others = pl.ds(0, n_ens - 1)
+    wait_for(border.at[near, others], border_recv.at[near])
     sum_border(near)
+    wait_for(border.at[near, others], border_send.at[near])
     for g in range(inner):
 
         @pl.when(me_e != owner(g))
@@ -253,7 +335,30 @@
 
     for side in (0, 1):
         wait_for(rim_out.at[side], rim_send.at[side])
-    sum_border(far)
+
+    @pl.when(giver)
+    def _():
+        for i, (mine, gift) in enumerate(gifts):
+            wait_for(gift.at[0], gift_send.at[i])
+        wait_for(border.at[0, 0:ROW], border_recv.at[0])
+
+    @pl.when(taker)
+    def _():
+        wait_for(border.at[0, 0 : ROW - 1], border_recv.at[0])
+
+    @pl.when(first)
+    def _():
+        sum_border(0, ROW)
+
+    @pl.when(taker)
+    def _():
+        wait_for(border.at[0, others], border_send.at[0])
+
+    @pl.when(jnp.logical_not(first))
+    def _():
+        wait_for(border.at[far, others], border_recv.at[far])
+        sum_border(far)
+        wait_for(border.at[far, others], border_send.at[far])
 
 
 def local(n_space, n_ens, members, field, weight, offsets):
@@ -279,6 +384,11 @@
             pltpu.VMEM((inner, RIM, ch, BS), jnp.float32),
             pltpu.VMEM((n_ens - 1, RIM, ch, BS), jnp.float32),
             pltpu.VMEM((2, n_ens, RIM, ch, BS), jnp.float32),
+            pltpu.VMEM((n_ens // ROW, RIM, rows, BS), jnp.bfloat16),
+            pltpu.VMEM((RIM, rows, BS), jnp.bfloat16),
+            pltpu.VMEM((n_ens // ROW - 1, RIM, rows, BS), jnp.bfloat16),
+            pltpu.VMEM((n_ens // ROW - 1, RIM, rows, BS), jnp.bfloat16),
+            pltpu.VMEM((n_ens // ROW - 1, RIM, rows, BS), jnp.bfloat16),
             dma((3,)),
             dma((3,)),
             dma((nb // RIM,)),
@@ -292,6 +402,9 @@
             dma((inner,)),
             dma((2,)),
             dma((2,)),
+            dma((n_ens // ROW,)),
+            dma((3,)),
+            dma((3, n_ens // ROW - 1)),
         ],
         compiler_params=pltpu.CompilerParams(
             collective_id=0, has_side_effects=True, vmem_limit_bytes=VMEM_LIMIT

time: 27.7 us -> 27.1 us (0.978)
  the two profiles are of different devices: /device:TPU:6 before, /device:TPU:64 now
where the time goes in v6:
time: 27.1 us; the launch traced here: 27 us
  Pallas kernels  26.3 us (97%)
  local copies, waits for them, and re-layouts  0.64 us (2%)
    pallas_call x1, Pallas kernels, local(): call(*(pltpu.with_memory_space_constraint(x, pltpu.HBM) for x in operands))  26.3 us
    unnamed x1, local copies, waits for them, and re-layouts  0.64 us

profile of v6, /device:TPU:64, one launch (start us, length us, event | category | flops | bytes accessed | tf_op | source)
XLA Modules:
  0.0 27.0 jit_solution(6391820230494472716)
XLA Ops:
  0.0 26.3 %shard_map.46 = f32[8,3072]{1,0:T(8,128)S(1)} custom-call(s32[4,24]{1,0:T(4,128)} %bitcast.5, bf16[64,3072]{1,0:T(8,128)(2,1)} %bitcast.4, bf16[8,3072]{1,0:T(8,128)(2,1)} %field_hbm.1, bf16[24,512,128]{2,1,0:T(8,128)(2,1)} %bitcast.3), custom_call_target="tpu_custom_call" | custom-call | flops 403000000 | bytes 3800000 | tf_op jit(solution)/shard_map/pallas_call | solution.py:420
  26.3 0.6 %copy.6 = f32[8,3072]{1,0:T(8,128)} copy(f32[8,3072]{1,0:T(8,128)S(1)} %shard_map.46) | data formatting | bytes 196608

commit v7 on v6

--- a/solution.py
+++ b/solution.py
@@ -243,8 +243,8 @@
             border[side, me_e, i] = forward(base + i)
         give_border(side)
 
-    def give_border(side):
-        for p in partners:
+    def give_border(side, order=partners):
+        for p in order:
             pltpu.make_async_remote_copy(
                 src_ref=border.at[side, me_e], dst_ref=border.at[side, me_e],
                 send_sem=border_send.at[side], recv_sem=border_recv.at[side],
@@ -290,11 +290,10 @@
 
     @pl.when(taker)
     def _():
-        def finish_row(r, _):
+        def finish_row(r):
             wait_for(rims.at[r], rims_recv.at[r])
 
-            @pl.when(r > 0)
-            def _():
+            if r > 0:
                 for i, (mine, gift) in enumerate(gifts):
                     wait_for(gift.at[r - 1], gift_recv.at[i, r - 1])
                 for b in range(RIM):
@@ -304,12 +303,14 @@
 
             spread[0:RIM] = (back[0:RIM] + rims[r].astype(jnp.float32)).astype(jnp.bfloat16)
             for i in range(RIM):
-                border[0, me_e, i] += forward(i)
-            return 0
-
-        border[0, me_e] = jnp.zeros_like(border[0, me_e])
-        lax.fori_loop(0, n_rows, finish_row, 0)
-        give_border(0)
+                if r == 0:
+                    border[0, me_e, i] = forward(i)
+                else:
+                    border[0, me_e, i] += forward(i)
+
+        for r in range(n_rows):
+            finish_row(r)
+        give_border(0, partners[ROW : 2 * ROW] + partners[2 * ROW :] + partners[:ROW])
 
     def sum_border(side, count=n_ens):
         total = border[side, 0]

time: 27.1 us -> 27 us (level)
  the two profiles are of different devices: /device:TPU:64 before, /device:TPU:2 now
where the time goes in v7:
time: 27 us; the launch traced here: 26.8 us
  Pallas kernels  26.1 us (97%)
  local copies, waits for them, and re-layouts  0.64 us (2%)
    pallas_call x1, Pallas kernels, local(): call(*(pltpu.with_memory_space_constraint(x, pltpu.HBM) for x in operands))  26.1 us
    unnamed x1, local copies, waits for them, and re-layouts  0.64 us

profile of v7, /device:TPU:2, one launch (start us, length us, event | category | flops | bytes accessed | tf_op | source)
XLA Modules:
  0.0 26.8 jit_solution(9433866620004606743)
XLA Ops:
  0.0 26.1 %shard_map.46 = f32[8,3072]{1,0:T(8,128)S(1)} custom-call(s32[4,24]{1,0:T(4,128)} %bitcast.5, bf16[64,3072]{1,0:T(8,128)(2,1)} %bitcast.4, bf16[8,3072]{1,0:T(8,128)(2,1)} %field_hbm.1, bf16[24,512,128]{2,1,0:T(8,128)(2,1)} %bitcast.3), custom_call_target="tpu_custom_call" | custom-call | flops 403000000 | bytes 3800000 | tf_op jit(solution)/shard_map/pallas_call | solution.py:421
  26.1 0.6 %copy.6 = f32[8,3072]{1,0:T(8,128)} copy(f32[8,3072]{1,0:T(8,128)S(1)} %shard_map.46) | data formatting | bytes 196608

commit v8 on v7

--- a/solution.py
+++ b/solution.py
@@ -138,8 +138,11 @@
         copy.wait()
     member_copies[chunks - 1].wait()
     weight_copies[chunks - 1].wait()
-    for c in order[2:]:
-        load(c)
+    def load_inner():
+        for c in order[2:]:
+            load(c)
+
+    pl.when(jnp.logical_not(last))(load_inner)
     for b in range(nb - RIM, nb):
         adjoint(b)
     rim_out[1] = back[nb : nb + RIM].astype(jnp.bfloat16)
@@ -172,6 +175,8 @@
     def _():
         send_rim(0)
         pl.semaphore_signal(ready.at[1], inc=1, device_id=(left, me_e), device_id_type=MESH)
+
+    pl.when(last)(load_inner)
 
     for p in cross:
         pl.semaphore_signal(met, inc=1, device_id=(me_s, p), device_id_type=MESH)

time: 27 us -> 27 us (level)
  no operation moved by 1% of the time
where the time goes in v8:
time: 27 us; the launch traced here: 26.8 us
  Pallas kernels  26.1 us (97%)
  local copies, waits for them, and re-layouts  0.64 us (2%)
    pallas_call x1, Pallas kernels, local(): call(*(pltpu.with_memory_space_constraint(x, pltpu.HBM) for x in operands))  26.1 us
    unnamed x1, local copies, waits for them, and re-layouts  0.64 us

profile of v8, /device:TPU:2, one launch (start us, length us, event | category | flops | bytes accessed | tf_op | source)
XLA Modules:
  0.0 26.8 jit_solution(1966712929599235003)
XLA Ops:
  0.0 26.1 %shard_map.46 = f32[8,3072]{1,0:T(8,128)S(1)} custom-call(s32[4,24]{1,0:T(4,128)} %bitcast.5, bf16[64,3072]{1,0:T(8,128)(2,1)} %bitcast.4, bf16[8,3072]{1,0:T(8,128)(2,1)} %field_hbm.1, bf16[24,512,128]{2,1,0:T(8,128)(2,1)} %bitcast.3), custom_call_target="tpu_custom_call" | custom-call | flops 403000000 | bytes 3800000 | tf_op jit(solution)/shard_map/pallas_call | solution.py:426
  26.1 0.6 %copy.6 = f32[8,3072]{1,0:T(8,128)} copy(f32[8,3072]{1,0:T(8,128)S(1)} %shard_map.46) | data formatting | bytes 196608
